TPU v7x, 256 devices: a whole 4x4x8 slice. The times are simulated.
256 devices in a mesh: dom: 128 (over y, z, x), samp: 2 (over core).
Axes of the slice: x: 4, y: 4, z: 8, core: 2. Of those that a mesh axis runs over, the one named last changes fastest.
Arguments:
- state: float32 [2, 32768, 256], P(None, 'dom', 'samp'), may hold values from -6 to 6
- demand_load: bfloat16 [2, 256, 16384], P('samp', 'dom'), may hold values from 0.099609375 to 2
- node_coef: float32 [2, 32768], P(None, 'dom'), may hold values from 0.2 to 2
- pipe_ends: int32 [2, 65536], P(None, 'dom'), may hold values from 0 to 255, as said below
- pipe_coef: float32 [2, 65536], P(None, 'dom'), may hold values from 0.5 to 2
- iface_node: int32 [128, 4, 64], P('dom'), may hold values from 0 to 255
- iface_coef: float32 [2, 128, 2, 64], replicated, may hold values from 0.5 to 2
- cons_node: int32 [128, 256], P('dom'), may hold values from 0 to 255
- cons_count: int32 [128], P('dom'), may hold values from 1 to 256, 16384 in all
Outputs:
- newton_step: float32 [2, 32768, 256], P(None, 'dom', 'samp')
- residual: float32 [2, 32768, 256], P(None, 'dom', 'samp')
Inputs may be any that keep to these rules, and one draw needn't show every extreme that they name: `pipe_ends`: the two ends of every interior pipe are different nodes of its partition.
All inputs are finite; a program needn't handle non-finite values. No bound on the sum of `cons_count` on one device may be relied on, other than what follows from the above.
Results may differ from a plain program's by a relative error of at most 0.0003.
Values may be sent and summed in bfloat16 or wider, within the bound.
A program may use at most 64 MiB of HBM per device.

v0:
```python
import jax
import jax.numpy as jnp
from jax import lax
from jax.experimental import pallas as pl
from jax.experimental.pallas import tpu as pltpu
from jax.sharding import PartitionSpec as P

ITERS = 4
REACH = 4
MESH = pl.DeviceIdType.MESH
F32 = jnp.float32
BF16 = jnp.bfloat16

NODES = 256
PIPES = 512
IFACE = 64
FACES = 4 * IFACE
WIDTH = 128
SLOTS = 128
N_DOM = 128
HALF_DOM = N_DOM // 2
PARTNER_COLOUR = (1, 0, 3, 2)


def split(value):
    high = value.astype(BF16)
    return high, (value - high.astype(F32)).astype(BF16)


def mm(table, value):
    return jnp.dot(table, value, preferred_element_type=F32)


def column(row):
    return jnp.transpose(jnp.broadcast_to(row, (WIDTH, row.shape[1])))


def two(left, right):
    return jnp.concatenate([left, right], axis=1)


def onehot(condition):
    return jnp.where(condition, F32(1.0), F32(0.0))


def pipe_terms(drop, temp_sum, temp_drop, conduct, spread):
    square = 1.0 + drop * drop
    half_power = lax.rsqrt(square)
    quarter = jnp.sqrt(half_power)
    flow = conduct * drop * quarter
    slope = conduct * (1.0 + 0.5 * drop * drop) * half_power * half_power * quarter
    under = flow * flow + spread * spread
    inverse = lax.rsqrt(under)
    half_flow = 0.5 * flow
    mixing = 0.5 * under * inverse
    heat = half_flow * temp_sum + mixing * temp_drop
    heat_slope = 0.5 * temp_sum + temp_drop * half_flow * inverse
    return flow, heat, slope, heat_slope * slope, half_flow, mixing


def kernel(
    state_hbm,
    demand_hbm,
    node_coef_hbm,
    pipe_ends_hbm,
    pipe_coef_hbm,
    iface_node_hbm,
    iface_coef_hbm,
    cons_node_hbm,
    cons_count_hbm,
    step_hbm,
    resid_hbm,
    state,
    demand,
    node_coef,
    pipe_ends,
    pipe_coef,
    iface_node,
    iface_coef,
    cons_node,
    cons_count,
    rows_in,
    rows,
    faces_out,
    faces_in,
    m_nodes,
    a_nodes,
    m_pipes,
    a_pipes,
    f_nodes,
    f_faces,
    inner,
    outer,
    node,
    serves,
    high,
    low,
    pipe_high,
    pipe_low,
    face_high,
    face_low,
    extra_high,
    extra_low,
    mixed_both,
    rho,
    delta,
    step,
    resid,
    load_sem,
    out_sem,
    rows_send,
    rows_self_send,
    rows_recv,
    face_send,
    face_recv,
):
    rank = lax.axis_index("dom")
    core = lax.axis_index("samp")
    owner_half = rank // HALF_DOM
    left = slice(0, WIDTH)
    right = slice(WIDTH, 2 * WIDTH)

    barrier = pltpu.get_barrier_semaphore()
    around = [lax.rem(rank + o + N_DOM, N_DOM) for o in (1, -1, REACH, -REACH)]
    for j in range(HALF_DOM):
        for c in range(2):
            pl.semaphore_signal(
                barrier,
                inc=1,
                device_id=(HALF_DOM * core + lax.rem(rank + j, HALF_DOM), c),
                device_id_type=MESH,
            )
    for q in around:
        pl.semaphore_signal(barrier, inc=1, device_id=(q, core), device_id_type=MESH)

    loads = [
        (iface_node_hbm, iface_node),
        (state_hbm, state),
        (demand_hbm, demand),
        (node_coef_hbm, node_coef),
        (pipe_ends_hbm, pipe_ends),
        (pipe_coef_hbm, pipe_coef),
        (cons_node_hbm, cons_node),
        (cons_count_hbm, cons_count),
        (iface_coef_hbm, iface_coef),
    ]
    loads = [
        pltpu.make_async_copy(src, dst, load_sem.at[i]) for i, (src, dst) in enumerate(loads)
    ]
    for load in loads:
        load.start()

    def chunk(i, size):
        return slice(i * size, (i + 1) * size)

    loads[0].wait()
    face_rows = [iface_node[0, c : c + 1, :].astype(F32) for c in range(4)]
    lane_of_node = lax.broadcasted_iota(jnp.int32, (IFACE, WIDTH), 1).astype(F32)
    for c in range(4):
        ids = column(face_rows[c])
        for part in range(NODES // WIDTH):
            f_faces[chunk(c, IFACE), chunk(part, WIDTH)] = onehot(
                ids == lane_of_node + float(part * WIDTH)
            ).astype(BF16)
    loads[1].wait()
    for i in range(2):
        for f in range(2):
            high[chunk(i, 128), chunk(f, WIDTH)], low[chunk(i, 128), chunk(f, WIDTH)] = split(
                state[f, chunk(i, 128), :]
            )

    def face_copies(turn):
        return [
            pltpu.make_async_remote_copy(
                src_ref=faces_out.at[turn, c],
                dst_ref=faces_in.at[turn, PARTNER_COLOUR[c]],
                send_sem=face_send.at[turn, c],
                recv_sem=face_recv.at[turn, PARTNER_COLOUR[c]],
                device_id=(around[c], core),
                device_id_type=MESH,
            )
            for c in range(4)
        ]

    def face_values(turn, c):
        table = f_faces[chunk(c, IFACE), :]
        faces_out[turn, c] = mm(table, high[...]) + mm(table, low[...])

    def pipe_drops(i):
        at = chunk(i, 128)
        drops = mm(m_pipes[at, :], high[...]) + mm(m_pipes[at, :], low[...])
        sums = mm(a_pipes[at, :], two(high[:, right], low[:, right]))
        return drops[:, left], drops[:, right], sums[:, left] + sums[:, right]

    copies = face_copies(0)
    for c in range(4):
        face_values(0, c)
    loads[2].wait()
    pl.semaphore_wait(barrier, N_DOM + 4)
    for copy in copies:
        copy.start()

    slot = core * HALF_DOM + lax.rem(rank, HALF_DOM)
    for k in range(1, N_DOM):
        p = lax.rem(rank + k, N_DOM)
        pltpu.make_async_remote_copy(
            src_ref=demand.at[0, :, pl.ds(pl.multiple_of(p * SLOTS, SLOTS), SLOTS)],
            dst_ref=rows_in.at[slot],
            send_sem=rows_send,
            recv_sem=rows_recv,
            device_id=(p, owner_half),
            device_id_type=MESH,
        ).start()
    own_rows = demand.at[0, :, pl.ds(pl.multiple_of(rank * SLOTS, SLOTS), SLOTS)]

    @pl.when(owner_half == core)
    def _():
        pltpu.make_async_copy(own_rows, rows_in.at[slot], rows_recv).start()

    across = pltpu.make_async_remote_copy(
        src_ref=own_rows,
        dst_ref=rows_in.at[slot],
        send_sem=rows_self_send,
        recv_sem=rows_recv,
        device_id=(rank, 1 - core),
        device_id_type=MESH,
    )

    @pl.when(owner_half != core)
    def _():
        across.start()

    for load in loads[3:]:
        load.wait()

    for i in range(NODES // 128):
        node_of_row = lax.broadcasted_iota(jnp.int32, (128, PIPES), 0) + i * 128
        at_start = onehot(pipe_ends[0:1, :] == node_of_row)
        at_end = onehot(pipe_ends[1:2, :] == node_of_row)
        m_nodes[chunk(i, 128), :] = (at_start - at_end).astype(BF16)
        a_nodes[chunk(i, 128), :] = (at_start + at_end).astype(BF16)
    lane_of_node = lax.broadcasted_iota(jnp.int32, (128, WIDTH), 1).astype(F32)
    for i in range(PIPES // 128):
        start_ids = column(pipe_ends[0:1, chunk(i, 128)].astype(F32))
        end_ids = column(pipe_ends[1:2, chunk(i, 128)].astype(F32))
        for part in range(NODES // WIDTH):
            at_start = onehot(start_ids == lane_of_node + float(part * WIDTH))
            at_end = onehot(end_ids == lane_of_node + float(part * WIDTH))
            m_pipes[chunk(i, 128), chunk(part, WIDTH)] = (at_start - at_end).astype(BF16)
            a_pipes[chunk(i, 128), chunk(part, WIDTH)] = (at_start + at_end).astype(BF16)
    face_ids = jnp.concatenate(face_rows, axis=1)
    for i in range(NODES // 128):
        node_of_row = lax.broadcasted_iota(jnp.int32, (128, FACES), 0) + i * 128
        f_nodes[chunk(i, 128), :] = onehot(face_ids == node_of_row.astype(F32)).astype(BF16)

    def scatter(table, i, upper, lower):
        return mm(table[chunk(i, 128), :], upper[...]) + mm(table[chunk(i, 128), :], lower[...])

    for i in range(PIPES // 128):
        at = chunk(i, 128)
        drop, temp_drop, temp_sum = pipe_drops(i)
        flow, heat, slope, mixed, half_flow, mixing = pipe_terms(
            drop, temp_sum, temp_drop, column(pipe_coef[0:1, at]), column(pipe_coef[1:2, at])
        )
        inner[0, at], inner[1, at], inner[2, at], inner[3, at] = slope, mixed, half_flow, mixing
        pipe_high[at, left], pipe_low[at, left] = split(flow)
        pipe_high[at, right], pipe_low[at, right] = split(heat)
        extra_high[at, left], extra_low[at, left] = split(slope)
        extra_high[at, right], extra_low[at, right] = split(mixing)
        mixed_both[at, left], mixed_both[at, right] = split(mixed)
    for i in range(NODES // 128):
        at = chunk(i, 128)
        rho[at, :] = scatter(m_nodes, i, pipe_high, pipe_low)
        slopes = scatter(a_nodes, i, extra_high, extra_low)
        cross = mm(a_nodes[at, :], mixed_both[...])
        node[0, at] = column(node_coef[0:1, at])
        node[1, at] = column(node_coef[1:2, at])
        node[2, at] = node[0, at] + slopes[:, left]
        node[3, at] = 0.5 * rho[at, left] + slopes[:, right]
        node[4, at] = cross[:, left] + cross[:, right]
        live = lax.broadcasted_iota(jnp.int32, (128, 2 * SLOTS), 1) < cons_count[...]
        here = cons_node[...] == lax.broadcasted_iota(jnp.int32, (128, 2 * SLOTS), 0) + i * 128
        serves[at, :] = onehot(jnp.logical_and(live, here)).astype(BF16)

    step[...] = jnp.zeros_like(step)

    lane = lax.broadcasted_iota(jnp.int32, (IFACE, N_DOM), 1)

    def iface_column(which, c):
        owner = (rank, around[1], rank, around[3])[c]
        mine = jnp.where(lane == owner, iface_coef[which, c // 2], F32(0.0))
        return jnp.broadcast_to(jnp.sum(mine, axis=1, keepdims=True), (IFACE, WIDTH))

    for c in range(4):
        outer[0, chunk(c, IFACE)] = iface_column(0, c)
        outer[1, chunk(c, IFACE)] = iface_column(1, c)
    for copy in copies:
        copy.wait_recv()
    for c in range(4):
        at = chunk(c, IFACE)
        near_head, near_temp = faces_out[0, c, :, left], faces_out[0, c, :, right]
        far_head, far_temp = faces_in[0, c, :, left], faces_in[0, c, :, right]
        flow, heat, slope, mixed, half_flow, mixing = pipe_terms(
            near_head - far_head, near_temp + far_temp, near_temp - far_temp, outer[0, at], outer[1, at]
        )
        upper = half_flow + mixing
        outer[0, at], outer[1, at], outer[2, at], outer[3, at] = slope, mixed, upper, half_flow - mixing
        face_high[at, left], face_low[at, left] = split(flow)
        face_high[at, right], face_low[at, right] = split(heat)
        extra_high[at, left], extra_low[at, left] = split(slope)
        extra_high[at, right], extra_low[at, right] = split(upper)
        mixed_both[at, left], mixed_both[at, right] = split(mixed)
    for i in range(NODES // 128):
        at = chunk(i, 128)
        rho[at, :] += scatter(f_nodes, i, face_high, face_low)
        table = f_nodes[at, :]
        slopes = mm(table, extra_high[:FACES, :]) + mm(table, extra_low[:FACES, :])
        cross = mm(table, mixed_both[:FACES, :])
        node[2, at] = 1.0 / (node[2, at] + slopes[:, left])
        node[3, at] += slopes[:, right]
        node[4, at] += cross[:, left] + cross[:, right]

    def precondition(i):
        at = chunk(i, 128)
        head = -rho[at, left] * node[2, at]
        temp = -(rho[at, right] + node[4, at] * head) * node[3, at]
        delta[at, left] = head
        delta[at, right] = temp
        high[at, left], low[at, left] = split(head)
        high[at, right], low[at, right] = split(temp)

    pltpu.make_async_remote_copy(
        src_ref=rows_in,
        dst_ref=rows_in,
        send_sem=rows_send,
        recv_sem=rows_recv,
        device_id=(rank, 1 - core),
        device_id_type=MESH,
    ).wait_recv()
    for h in range(2):
        for j in range(HALF_DOM):
            rows[2 * j : 2 * j + 2, chunk(h, SLOTS)] = rows_in[h * HALF_DOM + j].astype(F32)
    for i in range(NODES // 128):
        at = chunk(i, 128)
        usage = lax.dot_general(
            serves[at, :],
            rows[...].astype(BF16),
            (((1,), (1,)), ((), ())),
            preferred_element_type=F32,
        )
        cooling = node[1, at] + usage
        node[1, at] = cooling
        node[3, at] = 1.0 / (node[3, at] + cooling)
        rho[at, left] += node[0, at] * state[0, at] + usage
        rho[at, right] += cooling * state[1, at]
        resid[0, at] = rho[at, left]
        resid[1, at] = rho[at, right]
        precondition(i)

    resid_out = pltpu.make_async_copy(resid, resid_hbm, out_sem.at[0])
    resid_out.start()

    def one_turn(turn, carry):
        copies = face_copies(turn)
        for c in range(4):
            face_values(turn, c)
            copies[c].start()
        for i in range(PIPES // 128):
            at = chunk(i, 128)
            drop, temp_drop, temp_sum = pipe_drops(i)
            pipe_high[at, left], pipe_low[at, left] = split(inner[0, at] * drop)
            pipe_high[at, right], pipe_low[at, right] = split(
                inner[1, at] * drop + inner[2, at] * temp_sum + inner[3, at] * temp_drop
            )
        for c in range(4):
            at = chunk(c, IFACE)
            head, temp = faces_out[turn, c, :, left], faces_out[turn, c, :, right]
            face_high[at, left], face_low[at, left] = split(outer[0, at] * head)
            face_high[at, right], face_low[at, right] = split(outer[1, at] * head + outer[2, at] * temp)
        for i in range(NODES // 128):
            at = chunk(i, 128)
            moved = scatter(m_nodes, i, pipe_high, pipe_low) + scatter(f_nodes, i, face_high, face_low)
            head, temp = delta[at, left], delta[at, right]
            rho[at, left] += moved[:, left] + node[0, at] * head
            rho[at, right] += moved[:, right] + node[1, at] * temp
            step[0, at] += head
            step[1, at] += temp
        for copy in copies:
            copy.wait_recv()
        for c in range(4):
            at = chunk(c, IFACE)
            head, temp = faces_in[turn, c, :, left], faces_in[turn, c, :, right]
            face_high[at, left], face_low[at, left] = split(-outer[0, at] * head)
            face_high[at, right], face_low[at, right] = split(outer[3, at] * temp - outer[1, at] * head)
        for i in range(NODES // 128):
            at = chunk(i, 128)
            rho[at, :] += scatter(f_nodes, i, face_high, face_low)
            precondition(i)
        return carry

    lax.fori_loop(1, ITERS + 1, one_turn, 0)
    for i in range(NODES // 128):
        at = chunk(i, 128)
        step[0, at] += delta[at, left]
        step[1, at] += delta[at, right]
    step_out = pltpu.make_async_copy(step, step_hbm, out_sem.at[1])
    step_out.start()

    def sent(turn, carry):
        for copy in face_copies(turn):
            copy.wait_send()
        return carry

    lax.fori_loop(0, ITERS + 1, sent, 0)
    pltpu.make_async_remote_copy(
        src_ref=rows_in.at[pl.ds(0, N_DOM - 1)],
        dst_ref=rows_in.at[pl.ds(0, N_DOM - 1)],
        send_sem=rows_send,
        recv_sem=rows_recv,
        device_id=(rank, 1 - core),
        device_id_type=MESH,
    ).wait_send()

    @pl.when(owner_half != core)
    def _():
        across.wait_send()

    resid_out.wait()
    step_out.wait()


def shards(
    state,
    demand_load,
    node_coef,
    pipe_ends,
    pipe_coef,
    iface_node,
    iface_coef,
    cons_node,
    cons_count,
):
    vmem = pltpu.VMEM
    dma = pltpu.SemaphoreType.DMA
    anywhere = pl.BlockSpec(memory_space=pl.ANY)
    out = jax.ShapeDtypeStruct((2, NODES, WIDTH), F32)
    step, resid = pl.pallas_call(
        kernel,
        out_shape=(out, out),
        in_specs=[anywhere] * 9,
        out_specs=(anywhere, anywhere),
        scratch_shapes=[
            vmem((2, NODES, WIDTH), F32),
            vmem((1, 2, N_DOM * SLOTS), BF16),
            vmem((2, NODES), F32),
            vmem((2, PIPES), jnp.int32),
            vmem((2, PIPES), F32),
            vmem((1, 4, IFACE), jnp.int32),
            vmem((2, 2, IFACE, N_DOM), F32),
            vmem((1, 2 * SLOTS), jnp.int32),
            vmem((1, 1), jnp.int32),
            vmem((N_DOM, 2, SLOTS), BF16),
            vmem((WIDTH, 2 * SLOTS), F32),
            vmem((ITERS + 1, 4, IFACE, 2 * WIDTH), F32),
            vmem((ITERS + 1, 4, IFACE, 2 * WIDTH), F32),
            vmem((NODES, PIPES), BF16),
            vmem((NODES, PIPES), BF16),
            vmem((PIPES, NODES), BF16),
            vmem((PIPES, NODES), BF16),
            vmem((NODES, FACES), BF16),
            vmem((FACES, NODES), BF16),
            vmem((4, PIPES, WIDTH), F32),
            vmem((4, FACES, WIDTH), F32),
            vmem((5, NODES, WIDTH), F32),
            vmem((NODES, 2 * SLOTS), BF16),
            vmem((NODES, 2 * WIDTH), BF16),
            vmem((NODES, 2 * WIDTH), BF16),
            vmem((PIPES, 2 * WIDTH), BF16),
            vmem((PIPES, 2 * WIDTH), BF16),
            vmem((FACES, 2 * WIDTH), BF16),
            vmem((FACES, 2 * WIDTH), BF16),
            vmem((PIPES, 2 * WIDTH), BF16),
            vmem((PIPES, 2 * WIDTH), BF16),
            vmem((PIPES, 2 * WIDTH), BF16),
            vmem((NODES, 2 * WIDTH), F32),
            vmem((NODES, 2 * WIDTH), F32),
            vmem((2, NODES, WIDTH), F32),
            vmem((2, NODES, WIDTH), F32),
            dma((9,)),
            dma((2,)),
            dma,
            dma,
            dma,
            dma((ITERS + 1, 4)),
            dma((ITERS + 1, 4)),
        ],
        compiler_params=pltpu.CompilerParams(
            collective_id=0, has_side_effects=True, vmem_limit_bytes=56 << 20
        ),
        name="newton_step",
    )(
        state,
        demand_load,
        node_coef,
        pipe_ends,
        pipe_coef,
        iface_node,
        jnp.transpose(iface_coef, (0, 2, 3, 1)),
        cons_node,
        cons_count.reshape(1, 1),
    )
    return step, resid


def solution(mesh):
    placed = (
        P(None, "dom", "samp"),
        P("samp", "dom", None),
        P(None, "dom"),
        P(None, "dom"),
        P(None, "dom"),
        P("dom", None, None),
        P(),
        P("dom", None),
        P("dom"),
    )
    return jax.shard_map(
        shards,
        mesh=mesh,
        in_specs=placed,
        out_specs=(P(None, "dom", "samp"), P(None, "dom", "samp")),
        check_vma=False,
    )
```

profile of v0, /device:TPU:32, one launch (start us, length us, event | category | flops | bytes accessed | tf_op | source)
XLA Modules:
  0.0 53.2 jit_solution(18178459437710346225)
XLA Ops:
  1.3 49.5 %newton_step.1 = (f32[2,256,128]{2,1,0:T(8,128)}, f32[2,256,128]{2,1,0:T(8,128)}) custom-call(f32[2,256,128]{2,1,0:T(8,128)} %state_hbm.1, bf16[1,2,16384]{2,1,0:T(2,128)(2,1)} %demand_hbm.1, f32[2,256]{1,0:T(2,128)} %node_coef_hbm.1, s32[2,512]{1,0:T(2,128)} %pipe_ends_hbm.1, f32[2,512]{1,0:T(2,128)} %pipe_coef_hbm.1, s32[1,4,64]{2,1,0:T(4,128)} %iface_node_hbm.1, ...), custom_call_target="tpu_custom_call" | custom-call | tf_op jit(solution)/shard_map/newton_step/pallas_call | solution.py:447
  50.8 0.0 copy-start
  50.8 1.7 %copy.14 = f32[2,256,128]{2,1,0:T(8,128)} copy(f32[2,256,128]{2,1,0:T(8,128)} %get-tuple-element.4) | data formatting | bytes 524288
  52.5 0.0 copy-done
  52.5 0.7 %copy.15 = f32[2,256,128]{2,1,0:T(8,128)} copy(f32[2,256,128]{2,1,0:T(8,128)S(1)} %copy-done) | data formatting | bytes 524288
Async XLA Ops:
  50.8 1.7 %copy-start = (f32[2,256,128]{2,1,0:T(8,128)S(1)}, f32[2,256,128]{2,1,0:T(8,128)}, u32[]{:S(2)}) copy-start(f32[2,256,128]{2,1,0:T(8,128)} %get-tuple-element.5) | copy-start | bytes 786436
where the time goes:
time: 53.4 us; the launch traced here: 53.2 us
  Pallas kernels  49.5 us (93%)
  local copies, waits for them, and re-layouts  2.42 us (5%)
  between operations  1.3 us (2%)
    pallas_call x1, Pallas kernels, shards(): pl.pallas_call(kernel, out_shape=(out, out), in_specs=[anywhere] * 9, out...  49.5 us
    unnamed x4, local copies, waits for them, and re-layouts  2.42 us

commit v1 on v0

--- a/solution.py
+++ b/solution.py
@@ -20,6 +20,9 @@
 N_DOM = 128
 HALF_DOM = N_DOM // 2
 PARTNER_COLOUR = (1, 0, 3, 2)
+DEEP = 8
+FAR_FIRST_Z = (4, 3, 5, 2, 6, 1, 7, 0)
+FAR_FIRST_X = (2, 1, 3, 0)
 
 
 def split(value):
@@ -79,6 +82,7 @@
     iface_coef,
     cons_node,
     cons_count,
+    relay,
     rows_in,
     rows,
     faces_out,
@@ -108,6 +112,8 @@
     resid,
     load_sem,
     out_sem,
+    relay_send,
+    relay_recv,
     rows_send,
     rows_self_send,
     rows_recv,
@@ -120,16 +126,25 @@
     left = slice(0, WIDTH)
     right = slice(WIDTH, 2 * WIDTH)
 
+    at_y, at_z, at_x = rank // 32, lax.rem(rank // REACH, DEEP), lax.rem(rank, REACH)
+
+    def place(y, z, x):
+        return 32 * y + REACH * z + x
+
     barrier = pltpu.get_barrier_semaphore()
     around = [lax.rem(rank + o + N_DOM, N_DOM) for o in (1, -1, REACH, -REACH)]
-    for j in range(HALF_DOM):
-        for c in range(2):
-            pl.semaphore_signal(
-                barrier,
-                inc=1,
-                device_id=(HALF_DOM * core + lax.rem(rank + j, HALF_DOM), c),
-                device_id_type=MESH,
-            )
+    for dz in FAR_FIRST_Z[:-1]:
+        pl.semaphore_signal(
+            barrier,
+            inc=1,
+            device_id=(place(at_y, lax.rem(at_z + dz, DEEP), at_x), core),
+            device_id_type=MESH,
+        )
+    for dx in FAR_FIRST_X:
+        for y in range(2):
+            for c in range(2):
+                source = place(2 * core + y, at_z, lax.rem(at_x + dx, REACH))
+                pl.semaphore_signal(barrier, inc=1, device_id=(source, c), device_id_type=MESH)
     for q in around:
         pl.semaphore_signal(barrier, inc=1, device_id=(q, core), device_id_type=MESH)
 
@@ -196,39 +211,26 @@
     for c in range(4):
         face_values(0, c)
     loads[2].wait()
-    pl.semaphore_wait(barrier, N_DOM + 4)
+    pl.semaphore_wait(barrier, DEEP - 1 + 16 + 4)
+
+    def rows_of(y, z):
+        return demand.at[0, :, pl.ds(pl.multiple_of(place(y, z, 0) * SLOTS, SLOTS), REACH * SLOTS)]
+
+    for dz in FAR_FIRST_Z[:-1]:
+        z = lax.rem(at_z + dz, DEEP)
+        for y in range(4):
+            pltpu.make_async_remote_copy(
+                src_ref=rows_of(y, z),
+                dst_ref=relay.at[at_z, y],
+                send_sem=relay_send,
+                recv_sem=relay_recv,
+                device_id=(place(at_y, z, at_x), core),
+                device_id_type=MESH,
+            ).start()
     for copy in copies:
         copy.start()
-
-    slot = core * HALF_DOM + lax.rem(rank, HALF_DOM)
-    for k in range(1, N_DOM):
-        p = lax.rem(rank + k, N_DOM)
-        pltpu.make_async_remote_copy(
-            src_ref=demand.at[0, :, pl.ds(pl.multiple_of(p * SLOTS, SLOTS), SLOTS)],
-            dst_ref=rows_in.at[slot],
-            send_sem=rows_send,
-            recv_sem=rows_recv,
-            device_id=(p, owner_half),
-            device_id_type=MESH,
-        ).start()
-    own_rows = demand.at[0, :, pl.ds(pl.multiple_of(rank * SLOTS, SLOTS), SLOTS)]
-
-    @pl.when(owner_half == core)
-    def _():
-        pltpu.make_async_copy(own_rows, rows_in.at[slot], rows_recv).start()
-
-    across = pltpu.make_async_remote_copy(
-        src_ref=own_rows,
-        dst_ref=rows_in.at[slot],
-        send_sem=rows_self_send,
-        recv_sem=rows_recv,
-        device_id=(rank, 1 - core),
-        device_id_type=MESH,
-    )
-
-    @pl.when(owner_half != core)
-    def _():
-        across.start()
+    for y in range(4):
+        pltpu.make_async_copy(rows_of(y, at_z), relay.at[at_z, y], relay_recv).start()
 
     for load in loads[3:]:
         load.wait()
@@ -294,6 +296,50 @@
     for c in range(4):
         outer[0, chunk(c, IFACE)] = iface_column(0, c)
         outer[1, chunk(c, IFACE)] = iface_column(1, c)
+    pltpu.make_async_remote_copy(
+        src_ref=relay,
+        dst_ref=relay,
+        send_sem=relay_send,
+        recv_sem=relay_recv,
+        device_id=(rank, 1 - core),
+        device_id_type=MESH,
+    ).wait_recv()
+    group = core * 8 + lax.rem(at_y, 2) * REACH + at_x
+
+    def relayed(y, x):
+        return relay.at[:, y, :, pl.ds(pl.multiple_of(x * SLOTS, SLOTS), SLOTS)]
+
+    for dy in FAR_FIRST_X:
+        for dx in FAR_FIRST_X:
+            if (dy, dx) != (0, 0):
+                y, x = lax.rem(at_y + dy, 4), lax.rem(at_x + dx, REACH)
+                pltpu.make_async_remote_copy(
+                    src_ref=relayed(y, x),
+                    dst_ref=rows_in.at[group],
+                    send_sem=rows_send,
+                    recv_sem=rows_recv,
+                    device_id=(place(y, at_z, x), owner_half),
+                    device_id_type=MESH,
+                ).start()
+    own_rows = relayed(at_y, at_x)
+
+    @pl.when(owner_half == core)
+    def _():
+        pltpu.make_async_copy(own_rows, rows_in.at[group], rows_recv).start()
+
+    across = pltpu.make_async_remote_copy(
+        src_ref=own_rows,
+        dst_ref=rows_in.at[group],
+        send_sem=rows_self_send,
+        recv_sem=rows_recv,
+        device_id=(rank, 1 - core),
+        device_id_type=MESH,
+    )
+
+    @pl.when(owner_half != core)
+    def _():
+        across.start()
+
     for copy in copies:
         copy.wait_recv()
     for c in range(4):
@@ -338,8 +384,12 @@
         device_id_type=MESH,
     ).wait_recv()
     for h in range(2):
-        for j in range(HALF_DOM):
-            rows[2 * j : 2 * j + 2, chunk(h, SLOTS)] = rows_in[h * HALF_DOM + j].astype(F32)
+        for y in range(2):
+            for z in range(DEEP):
+                for x in range(REACH):
+                    rows[chunk(place(y, z, x), 2), chunk(h, SLOTS)] = rows_in[
+                        h * 8 + y * REACH + x, z
+                    ].astype(F32)
     for i in range(NODES // 128):
         at = chunk(i, 128)
         usage = lax.dot_general(
@@ -413,8 +463,16 @@
 
     lax.fori_loop(0, ITERS + 1, sent, 0)
     pltpu.make_async_remote_copy(
-        src_ref=rows_in.at[pl.ds(0, N_DOM - 1)],
-        dst_ref=rows_in.at[pl.ds(0, N_DOM - 1)],
+        src_ref=relay.at[pl.ds(0, DEEP - 1)],
+        dst_ref=relay.at[pl.ds(0, DEEP - 1)],
+        send_sem=relay_send,
+        recv_sem=relay_recv,
+        device_id=(rank, 1 - core),
+        device_id_type=MESH,
+    ).wait_send()
+    pltpu.make_async_remote_copy(
+        src_ref=rows_in.at[pl.ds(0, 15)],
+        dst_ref=rows_in.at[pl.ds(0, 15)],
         send_sem=rows_send,
         recv_sem=rows_recv,
         device_id=(rank, 1 - core),
@@ -459,7 +517,8 @@
             vmem((2, 2, IFACE, N_DOM), F32),
             vmem((1, 2 * SLOTS), jnp.int32),
             vmem((1, 1), jnp.int32),
-            vmem((N_DOM, 2, SLOTS), BF16),
+            vmem((DEEP, 4, 2, REACH * SLOTS), BF16),
+            vmem((16, DEEP, 2, SLOTS), BF16),
             vmem((WIDTH, 2 * SLOTS), F32),
             vmem((ITERS + 1, 4, IFACE, 2 * WIDTH), F32),
             vmem((ITERS + 1, 4, IFACE, 2 * WIDTH), F32),
@@ -491,6 +550,8 @@
             dma,
             dma,
             dma,
+            dma,
+            dma,
             dma((ITERS + 1, 4)),
             dma((ITERS + 1, 4)),
         ],

time: 53.4 us -> 50 us (0.936)
  the two profiles are of different devices: /device:TPU:32 before, /device:TPU:6 now
where the time goes in v1:
time: 50 us; the launch traced here: 49.9 us
  Pallas kernels  46.2 us (92%)
  local copies, waits for them, and re-layouts  2.42 us (5%)
  between operations  1.3 us (3%)
    pallas_call x1, Pallas kernels, shards(): pl.pallas_call(kernel, out_shape=(out, out), in_specs=[anywhere] * 9, out...  46.2 us
    unnamed x4, local copies, waits for them, and re-layouts  2.42 us

profile of v1, /device:TPU:6, one launch (start us, length us, event | category | flops | bytes accessed | tf_op | source)
XLA Modules:
  0.0 49.9 jit_solution(9714337555492200366)
XLA Ops:
  1.3 46.2 %newton_step.1 = (f32[2,256,128]{2,1,0:T(8,128)}, f32[2,256,128]{2,1,0:T(8,128)}) custom-call(f32[2,256,128]{2,1,0:T(8,128)} %state_hbm.1, bf16[1,2,16384]{2,1,0:T(2,128)(2,1)} %demand_hbm.1, f32[2,256]{1,0:T(2,128)} %node_coef_hbm.1, s32[2,512]{1,0:T(2,128)} %pipe_ends_hbm.1, f32[2,512]{1,0:T(2,128)} %pipe_coef_hbm.1, s32[1,4,64]{2,1,0:T(4,128)} %iface_node_hbm.1, ...), custom_call_target="tpu_custom_call" | custom-call | tf_op jit(solution)/shard_map/newton_step/pallas_call | solution.py:505
  47.5 0.0 copy-start
  47.5 1.7 %copy.14 = f32[2,256,128]{2,1,0:T(8,128)} copy(f32[2,256,128]{2,1,0:T(8,128)} %get-tuple-element.4) | data formatting | bytes 524288
  49.2 0.0 copy-done
  49.2 0.7 %copy.15 = f32[2,256,128]{2,1,0:T(8,128)} copy(f32[2,256,128]{2,1,0:T(8,128)S(1)} %copy-done) | data formatting | bytes 524288
Async XLA Ops:
  47.5 1.7 %copy-start = (f32[2,256,128]{2,1,0:T(8,128)S(1)}, f32[2,256,128]{2,1,0:T(8,128)}, u32[]{:S(2)}) copy-start(f32[2,256,128]{2,1,0:T(8,128)} %get-tuple-element.5) | copy-start | bytes 786436

commit v2 on v1

--- a/solution.py
+++ b/solution.py
@@ -485,6 +485,25 @@
 
     resid_out.wait()
     step_out.wait()
+
+
+def write_out(step_in, resid_in, step_out, resid_out, stage, in_sem, out_sem):
+    pairs = [(resid_in, resid_out, 0), (resid_in, resid_out, 1), (step_in, step_out, 0), (step_in, step_out, 1)]
+    fetches = [
+        pltpu.make_async_copy(src.at[f], stage.at[i], in_sem.at[i])
+        for i, (src, _, f) in enumerate(pairs)
+    ]
+    stores = [
+        pltpu.make_async_copy(stage.at[i], dst.at[f], out_sem.at[i])
+        for i, (_, dst, f) in enumerate(pairs)
+    ]
+    for fetch in fetches:
+        fetch.start()
+    for fetch, store in zip(fetches, stores):
+        fetch.wait()
+        store.start()
+    for store in stores:
+        store.wait()
 
 
 def shards(
@@ -570,6 +589,19 @@
         cons_node,
         cons_count.reshape(1, 1),
     )
+    step, resid = pl.pallas_call(
+        write_out,
+        out_shape=(out, out),
+        in_specs=[anywhere] * 2,
+        out_specs=(anywhere, anywhere),
+        scratch_shapes=[
+            vmem((4, NODES, WIDTH), F32),
+            dma((4,)),
+            dma((4,)),
+        ],
+        compiler_params=pltpu.CompilerParams(vmem_limit_bytes=56 << 20),
+        name="write_out",
+    )(step, resid)
     return step, resid
 
 

time: 50 us -> 49.4 us (0.988)
  local copies, waits for them, and re-layouts: 2.42 us -> 0 us
  Pallas kernels: 46.2 us -> 48 us
    unnamed x4 -> x0, local copies, waits for them, and re-layouts: 2.42 us -> none
    pallas_call x0 -> x1, Pallas kernels: none -> 1.82 us  [shards(): pl.pallas_call(write_out, out_shape=(out, out), in_specs=[anywhere] * 2,...]
where the time goes in v2:
time: 49.4 us; the launch traced here: 49.3 us
  Pallas kernels  48 us (97%)
  between operations  1.29 us (3%)
    pallas_call x1, Pallas kernels, shards(): pl.pallas_call(kernel, out_shape=(out, out), in_specs=[anywhere] * 9, out...  46.2 us
    pallas_call x1, Pallas kernels, shards(): pl.pallas_call(write_out, out_shape=(out, out), in_specs=[anywhere] * 2,...  1.82 us

profile of v2, /device:TPU:6, one launch (start us, length us, event | category | flops | bytes accessed | tf_op | source)
XLA Modules:
  0.0 49.3 jit_solution(7248060083600244054)
XLA Ops:
  1.3 46.2 %newton_step.1 = (f32[2,256,128]{2,1,0:T(8,128)}, f32[2,256,128]{2,1,0:T(8,128)}) custom-call(f32[2,256,128]{2,1,0:T(8,128)} %state_hbm.1, bf16[1,2,16384]{2,1,0:T(2,128)(2,1)} %demand_hbm.1, f32[2,256]{1,0:T(2,128)} %node_coef_hbm.1, s32[2,512]{1,0:T(2,128)} %pipe_ends_hbm.1, f32[2,512]{1,0:T(2,128)} %pipe_coef_hbm.1, s32[1,4,64]{2,1,0:T(4,128)} %iface_node_hbm.1, ...), custom_call_target="tpu_custom_call" | custom-call | tf_op jit(solution)/shard_map/newton_step/pallas_call | solution.py:524
  47.5 1.8 %write_out.1 = (f32[2,256,128]{2,1,0:T(8,128)}, f32[2,256,128]{2,1,0:T(8,128)}) custom-call(f32[2,256,128]{2,1,0:T(8,128)} %get-tuple-element.4.step_in, f32[2,256,128]{2,1,0:T(8,128)} %get-tuple-element.5.resid_in), custom_call_target="tpu_custom_call" | custom-call | tf_op jit(solution)/shard_map/write_out/pallas_call | solution.py:592

commit v3 on v2

--- a/solution.py
+++ b/solution.py
@@ -410,11 +410,31 @@
     resid_out = pltpu.make_async_copy(resid, resid_hbm, out_sem.at[0])
     resid_out.start()
 
+    wraps_x = (at_x == 0).astype(jnp.int32)
+    wraps_z = (at_z == 0).astype(jnp.int32)
+    leaving = [
+        (colour, lax.rem(rank + (1 - 2 * lax.rem(colour, 2)) * reach + N_DOM, N_DOM))
+        for colour, reach in (
+            (wraps_x, 1),
+            (2 + wraps_z, REACH),
+            (1 - wraps_x, 1),
+            (3 - wraps_z, REACH),
+        )
+    ]
+
     def one_turn(turn, carry):
         copies = face_copies(turn)
-        for c in range(4):
-            face_values(turn, c)
-            copies[c].start()
+        for colour, target in leaving:
+            table = f_faces[pl.ds(pl.multiple_of(colour * IFACE, IFACE), IFACE), :]
+            faces_out[turn, colour] = mm(table, high[...]) + mm(table, low[...])
+            pltpu.make_async_remote_copy(
+                src_ref=faces_out.at[turn, colour],
+                dst_ref=faces_in.at[turn, colour + 1 - 2 * lax.rem(colour, 2)],
+                send_sem=face_send.at[turn, colour],
+                recv_sem=face_recv.at[turn, colour + 1 - 2 * lax.rem(colour, 2)],
+                device_id=(target, core),
+                device_id_type=MESH,
+            ).start()
         for i in range(PIPES // 128):
             at = chunk(i, 128)
             drop, temp_drop, temp_sum = pipe_drops(i)

time: 49.4 us -> 48.9 us (0.990)
  Pallas kernels: 48 us -> 47.4 us
    pallas_call x1, Pallas kernels: 46.2 us -> 45.6 us  [shards(): pl.pallas_call(kernel, out_shape=(out, out), in_specs=[anywhere] * 9, out...]
where the time goes in v3:
time: 48.9 us; the launch traced here: 48.7 us
  Pallas kernels  47.4 us (97%)
  between operations  1.29 us (3%)
    pallas_call x1, Pallas kernels, shards(): pl.pallas_call(kernel, out_shape=(out, out), in_specs=[anywhere] * 9, out...  45.6 us
    pallas_call x1, Pallas kernels, shards(): pl.pallas_call(write_out, out_shape=(out, out), in_specs=[anywhere] * 2,...  1.82 us

profile of v3, /device:TPU:6, one launch (start us, length us, event | category | flops | bytes accessed | tf_op | source)
XLA Modules:
  0.0 48.7 jit_solution(11386981988404820228)
XLA Ops:
  1.3 45.6 %newton_step.1 = (f32[2,256,128]{2,1,0:T(8,128)}, f32[2,256,128]{2,1,0:T(8,128)}) custom-call(f32[2,256,128]{2,1,0:T(8,128)} %state_hbm.1, bf16[1,2,16384]{2,1,0:T(2,128)(2,1)} %demand_hbm.1, f32[2,256]{1,0:T(2,128)} %node_coef_hbm.1, s32[2,512]{1,0:T(2,128)} %pipe_ends_hbm.1, f32[2,512]{1,0:T(2,128)} %pipe_coef_hbm.1, s32[1,4,64]{2,1,0:T(4,128)} %iface_node_hbm.1, ...), custom_call_target="tpu_custom_call" | custom-call | tf_op jit(solution)/shard_map/newton_step/pallas_call | solution.py:544
  46.9 1.8 %write_out.1 = (f32[2,256,128]{2,1,0:T(8,128)}, f32[2,256,128]{2,1,0:T(8,128)}) custom-call(f32[2,256,128]{2,1,0:T(8,128)} %get-tuple-element.4.step_in, f32[2,256,128]{2,1,0:T(8,128)} %get-tuple-element.5.resid_in), custom_call_target="tpu_custom_call" | custom-call | tf_op jit(solution)/shard_map/write_out/pallas_call | solution.py:612

commit v4 on v3

--- a/solution.py
+++ b/solution.py
@@ -227,8 +227,6 @@
                 device_id=(place(at_y, z, at_x), core),
                 device_id_type=MESH,
             ).start()
-    for copy in copies:
-        copy.start()
     for y in range(4):
         pltpu.make_async_copy(rows_of(y, at_z), relay.at[at_z, y], relay_recv).start()
 
@@ -257,6 +255,9 @@
 
     def scatter(table, i, upper, lower):
         return mm(table[chunk(i, 128), :], upper[...]) + mm(table[chunk(i, 128), :], lower[...])
+
+    for copy in copies:
+        copy.start()
 
     for i in range(PIPES // 128):
         at = chunk(i, 128)

time: 48.9 us -> 48.6 us (level)
  no operation moved by 1% of the time
where the time goes in v4:
time: 48.6 us; the launch traced here: 48.5 us
  Pallas kernels  47.2 us (97%)
  between operations  1.29 us (3%)
    pallas_call x1, Pallas kernels, shards(): pl.pallas_call(kernel, out_shape=(out, out), in_specs=[anywhere] * 9, out...  45.4 us
    pallas_call x1, Pallas kernels, shards(): pl.pallas_call(write_out, out_shape=(out, out), in_specs=[anywhere] * 2,...  1.82 us

profile of v4, /device:TPU:6, one launch (start us, length us, event | category | flops | bytes accessed | tf_op | source)
XLA Modules:
  0.0 48.5 jit_solution(10270557069713187301)
XLA Ops:
  1.3 45.4 %newton_step.1 = (f32[2,256,128]{2,1,0:T(8,128)}, f32[2,256,128]{2,1,0:T(8,128)}) custom-call(f32[2,256,128]{2,1,0:T(8,128)} %state_hbm.1, bf16[1,2,16384]{2,1,0:T(2,128)(2,1)} %demand_hbm.1, f32[2,256]{1,0:T(2,128)} %node_coef_hbm.1, s32[2,512]{1,0:T(2,128)} %pipe_ends_hbm.1, f32[2,512]{1,0:T(2,128)} %pipe_coef_hbm.1, s32[1,4,64]{2,1,0:T(4,128)} %iface_node_hbm.1, ...), custom_call_target="tpu_custom_call" | custom-call | tf_op jit(solution)/shard_map/newton_step/pallas_call | solution.py:545
  46.6 1.8 %write_out.1 = (f32[2,256,128]{2,1,0:T(8,128)}, f32[2,256,128]{2,1,0:T(8,128)}) custom-call(f32[2,256,128]{2,1,0:T(8,128)} %get-tuple-element.4.step_in, f32[2,256,128]{2,1,0:T(8,128)} %get-tuple-element.5.resid_in), custom_call_target="tpu_custom_call" | custom-call | tf_op jit(solution)/shard_map/write_out/pallas_call | solution.py:613
